TPU v7x, 768 devices: a whole 4x8x12 slice. The times are simulated.
768 devices in a mesh: row: 96 (over y, z), col: 8 (over x, core).
Axes of the slice: x: 4, y: 8, z: 12, core: 2. Of those that a mesh axis runs over, the one named last changes fastest.
Arguments:
- confidences: bfloat16 [18432, 128, 128], P(('row', 'col')), may hold values from 0 to 40, as said below
- block_rows: int32 [18432], P(('row', 'col')), may hold values from 0 to 1
- block_cols: int32 [18432], P(('row', 'col')), may hold values from 0 to 23
- item_owner: int32 [48], replicated, may hold values from 0 to 7, as said below
- item_factors: bfloat16 [6144, 256], P('col'), may hold values from -0.375 to 0.375
- user_factors: float32 [24576, 256], P('row'), may hold values from -6 to 6
Outputs:
- new_factors: float32 [24576, 256], P('row')
Inputs may be any that keep to these rules, and one draw needn't show every extreme that they name: `item_owner`: of the 6 item blocks of one storage shard at most 3 name the same column group; one column group is named by exactly 3 blocks of every shard; every column group is named. `confidences`: Zero, or between 0.5 and 40.
All inputs are finite; a program needn't handle non-finite values.
Results may differ from a plain program's by a relative error of at most 0.01.
The roundings to bfloat16 on the way count: a program that leaves them out, or rounds other values in their place, can miss the bound.
Values may be sent and summed in bfloat16 or wider, within the bound.
A program may use at most 32 MiB of HBM per device.

v0:
```python
import jax
import jax.numpy as jnp
from jax import lax
from jax.sharding import PartitionSpec as P

CG_STEPS = 3


regular = 1.0
epsilon = 1e-06


def conjugate(solution, residual, apply_operator):
    direction = residual
    squares = jnp.sum(residual * residual, axis=1)
    for sweep in range(CG_STEPS):
        image = apply_operator(direction)
        step_size = squares / (jnp.sum(direction * image, axis=1) + epsilon)
        solution = solution + step_size[:, None] * direction
        residual = residual - step_size[:, None] * image
        if sweep + 1 < CG_STEPS:
            fresh = jnp.sum(residual * residual, axis=1)
            direction = residual + (fresh / (squares + epsilon))[:, None] * direction
            squares = fresh
    return solution


def local(confidences, block_rows, block_cols, item_owner, item_factors, user_factors):
    tile = confidences.shape[1]
    widths = item_factors.shape[1]
    all_blocks = item_owner.shape[0]
    column = lax.axis_index("col")
    user_count = user_factors.shape[0]
    slab_blocks = user_count // tile
    mine = (item_owner == column).astype(jnp.int32)
    ranking = jnp.cumsum(mine) - 1
    wanted = block_cols % jnp.sum(mine)
    matches = (mine[None, :] == 1) & (ranking[None, :] == wanted[:, None])
    global_ids = jnp.argmax(matches.astype(jnp.int32), axis=1)
    whole = lax.all_gather(item_factors, "col", axis=0, tiled=True).reshape(
        all_blocks, tile, widths
    )
    item_tiles = jnp.take(whole, global_ids, axis=0)
    dims = (((0,), (0,)), ((), ()))
    piece_rows = item_factors.shape[0] // lax.axis_size("row")
    item_piece = lax.dynamic_slice_in_dim(
        item_factors, lax.axis_index("row") * piece_rows, piece_rows, 0
    )
    local_gram = lax.dot_general(item_piece, item_piece, dims, preferred_element_type=jnp.float32)
    gram_matrix = lax.psum(local_gram, ("row", "col"))
    onehot = (block_rows[:, None] == jnp.arange(slab_blocks, dtype=jnp.int32)[None, :]).astype(
        jnp.float32
    )
    weights = confidences.astype(jnp.float32)

    def segment_total(contrib):
        totals = jnp.einsum("nb,nuk->buk", onehot, contrib, precision=lax.Precision.HIGHEST)
        return totals.reshape(user_count, widths)

    def block_term(rounded):
        user_tiles = jnp.take(rounded.reshape(slab_blocks, tile, widths), block_rows, axis=0)
        scores = jnp.einsum(
            "nuk,nik->nui", user_tiles, item_tiles, preferred_element_type=jnp.float32
        )
        weighted = (scores * weights).astype(jnp.bfloat16)
        contrib = jnp.einsum(
            "nui,nik->nuk", weighted, item_tiles, preferred_element_type=jnp.float32
        )
        return segment_total(contrib)

    preference = jnp.where(weights > 0, 1.0 + weights, 0.0).astype(jnp.bfloat16)
    rhs_part = segment_total(
        jnp.einsum("nui,nik->nuk", preference, item_tiles, preferred_element_type=jnp.float32)
    )
    first_part = rhs_part - block_term(user_factors.astype(jnp.bfloat16))

    def gram_apply(values):
        return jnp.dot(
            values, gram_matrix, precision=lax.Precision.HIGHEST, preferred_element_type=jnp.float32
        )

    def summed(partial_value):
        return lax.psum(partial_value, "col")

    def apply_full(direction):
        return (
            summed(block_term(direction.astype(jnp.bfloat16)))
            + gram_apply(direction)
            + regular * direction
        )

    residual = summed(first_part) - gram_apply(user_factors) - regular * user_factors
    return conjugate(user_factors, residual, apply_full)


def solution(mesh):
    in_specs = (
        P(("row", "col"), None, None),
        P(("row", "col")),
        P(("row", "col")),
        P(),
        P("col", None),
        P("row", None),
    )
    out_specs = P("row", None)
    return jax.shard_map(local, mesh=mesh, in_specs=in_specs, out_specs=out_specs, check_vma=False)
```

profile of v0, /device:TPU:1, one launch (start us, length us, event | category | flops | bytes accessed | tf_op | source)
XLA Modules:
  0.0 832.3 jit_solution(11724945892336814893)
XLA Ops:
  8.2 1.7 fusion.70
  17.3 1.9 gather_fusion.1
  19.1 35.6 %all-gather.2.cloned.1.call-done = bf16[6144,256]{1,0:T(8,128)(2,1)} async-done(((bf16[768,256]{1,0:T(8,128)(2,1)}), bf16[6144,256]{1,0:T(8,128)(2,1)}) %all-gather.2.cloned.1.call-update) | async-done | bytes 3145744 | tf_op jit(solution)/shard_map/all_gather | solution.py:40
  54.8 3.7 gather_fusion
  58.5 2.3 fusion.58
  60.8 5.4 fusion.46
  66.2 4.7 fusion.6
  70.9 2.9 fusion.48
  74.8 408.5 %all-reduce.8.cloned.1.call-done = f32[256,256]{1,0:T(8,128)} async-done(((f32[256,256]{1,0:T(8,128)}), f32[256,256]{1,0:T(8,128)}) %all-reduce.8.cloned.1.call-update) | async-done | bytes 262160 | tf_op jit(solution)/shard_map/psum | solution.py:50
  483.4 75.0 %all-reduce.6.cloned.1.call-done = f32[256,256]{1,0:T(8,128)} async-done(((f32[256,256]{1,0:T(8,128)}), f32[256,256]{1,0:T(8,128)}) %all-reduce.6.cloned.1.call-update) | async-done | bytes 262160 | tf_op jit(solution)/shard_map/psum | solution.py:83
  558.4 1.4 fusion.97
  559.8 1.9 gather_fusion.2
  561.7 4.2 fusion.43
  565.9 4.7 fusion.4
  571.4 74.7 %all-reduce.10.cloned.1.call-done = f32[256,256]{1,0:T(8,128)} async-done(((f32[256,256]{1,0:T(8,128)}), f32[256,256]{1,0:T(8,128)}) %all-reduce.10.cloned.1.call-update) | async-done | bytes 262160 | tf_op jit(solution)/shard_map/psum | solution.py:83
  646.1 1.4 multiply_reduce_fusion.3
  647.9 1.8 gather_fusion.3
  649.7 4.4 fusion.40
  654.1 4.7 fusion.2
  659.8 74.5 %all-reduce.12.cloned.1.call-done = f32[256,256]{1,0:T(8,128)} async-done(((f32[256,256]{1,0:T(8,128)}), f32[256,256]{1,0:T(8,128)}) %all-reduce.12.cloned.1.call-update) | async-done | bytes 262160 | tf_op jit(solution)/shard_map/psum | solution.py:83
  736.0 1.8 gather_fusion.4
  737.9 4.4 fusion.37
  742.2 4.7 fusion
  747.7 74.7 %all-reduce.14.cloned.1.call-done = f32[256,256]{1,0:T(8,128)} async-done(((f32[256,256]{1,0:T(8,128)}), f32[256,256]{1,0:T(8,128)}) %all-reduce.14.cloned.1.call-update) | async-done | bytes 262160 | tf_op jit(solution)/shard_map/psum | solution.py:83
  (51 shorter events, 14.7 us)
Async XLA Ops:
  7.4 47.4 %all-gather.2.cloned.1.call-start = ((), (), s32[]{:S(2)}) async-start(), calls=%async_computation | async-start | bytes 3538944 | tf_op jit(solution)/shard_map/all_gather | solution.py:40
  8.1 475.3 %all-reduce.8.cloned.1.call-start = ((), (), s32[]{:S(2)}) async-start(), calls=%async_computation.2 | async-start | bytes 524288 | tf_op jit(solution)/shard_map/psum | solution.py:50
  9.9 548.5 %all-reduce.6.cloned.1.call-start = ((), (), s32[]{:S(2)}) async-start(), calls=%async_computation.1 | async-start | bytes 524288 | tf_op jit(solution)/shard_map/psum | solution.py:83
  60.8 5.4 copy-start.4
  70.9 487.4 %copy-start.2 = (f32[256,256]{1,0:T(8,128)S(1)}, f32[256,256]{1,0:T(8,128)}, u32[]{:S(2)}) copy-start(f32[256,256]{1,0:T(8,128)} %param.13) | copy-start | bytes 786436
  74.6 571.5 %all-reduce.10.cloned.1.call-start = ((), (), s32[]{:S(2)}) async-start(), calls=%async_computation.3 | async-start | bytes 524288 | tf_op jit(solution)/shard_map/psum | solution.py:83
  559.8 1.9 copy-start
  559.8 1.9 copy-start.3
  565.9 80.2 %copy-start.1 = (f32[256,256]{1,0:T(8,128)S(1)}, f32[256,256]{1,0:T(8,128)}, u32[]{:S(2)}) copy-start(f32[256,256]{1,0:T(8,128)} %all-reduce.8.cloned.1.call-done) | copy-start | bytes 786436
  571.3 162.9 %all-reduce.12.cloned.1.call-start = ((), (), s32[]{:S(2)}) async-start(), calls=%async_computation.4 | async-start | bytes 524288 | tf_op jit(solution)/shard_map/psum | solution.py:83
  659.5 162.9 %all-reduce.14.cloned.1.call-start = ((), (), s32[]{:S(2)}) async-start(), calls=%async_computation.5 | async-start | bytes 524288 | tf_op jit(solution)/shard_map/psum | solution.py:83
Sparse Core Ops, SparseCore 0:
  10.9 43.8 all-gather.1
Sparse Core Ops, SparseCore 1:
  14.0 469.4 all-reduce.7
  485.7 72.6 all-reduce.5
  571.4 74.6 all-reduce.9
  659.6 74.6 all-reduce.11
  747.7 74.6 all-reduce.13
where the time goes:
time: 833 us; the launch traced here: 832 us
  waiting for transfers between devices  744 us (89%)
  matrix products  49.7 us (6%)
  between operations  16.5 us (2%)
  local copies, waits for them, and re-layouts  14.2 us (2%)
    psum x1, waiting for transfers between devices, local(): gram_matrix = lax.psum(local_gram, ('row', 'col'))  409 us
    psum x4, waiting for transfers between devices, summed(): return lax.psum(partial_value, 'col')  299 us
    all_gather x1, waiting for transfers between devices, local(): lax.all_gather(item_factors, 'col', axis=0, tiled=True)  35.6 us
    dot_general x5, matrix products, segment_total(): jnp.einsum('nb,nuk->buk', onehot, contrib, precision=lax.Precision.HIGHEST)  21.7 us
    dot_general x4, matrix products, block_term(): jnp.einsum('nui,nik->nuk', weighted, item_tiles, preferred_element_type=j...  18.2 us
  transfers between devices with their start and end apart: 6, of which 6 were waited for; matrix products, arithmetic and copies ran while one was open for 4% of the time, Pallas kernels for 0%

commit v1 on v0

v1 whole, which is shorter than its diff:
```python
import jax
import jax.numpy as jnp
from jax import lax
from jax.experimental import pallas as pl
from jax.experimental.pallas import tpu as pltpu
from jax.sharding import PartitionSpec as P

CG_STEPS = 3
Z_CHIPS = 12
Y_CHIPS = 8
X_CHIPS = 4
COLORS = 4

regular = 1.0
epsilon = 1e-06

MESH = pl.DeviceIdType.MESH
F32 = jnp.float32
BF16 = jnp.bfloat16


def kernel(
    conf_ref,
    rows_ref,
    cols_ref,
    owner_ref,
    items_ref,
    users_ref,
    out_ref,
    y_buf,
    conf_buf,
    pick_buf,
    wide,
    c_buf,
    p_buf,
    mine,
    result,
    local_sem,
    send_sem,
    recv_sem,
):
    n_blocks, tile = conf_ref.shape[0], conf_ref.shape[2]
    stored = items_ref.shape[0]
    n_items, width = y_buf.shape
    all_blocks = owner_ref.shape[0]
    n_col = n_items // stored
    part = tile // n_col
    total = n_blocks * n_col
    users = 2 * part

    row = lax.axis_index("row")
    me = lax.axis_index("col")
    x, core = me // 2, me % 2
    y, z = row // Z_CHIPS, row % Z_CHIPS
    color = (y + 2 * z) % COLORS

    def chip(dx):
        return (x + dx) % X_CHIPS

    def on_x(dx):
        return (row, 2 * chip(dx) + core)

    y_next = (((y + 1) % Y_CHIPS) * Z_CHIPS + z, me)
    y_prev = (((y + Y_CHIPS - 1) % Y_CHIPS) * Z_CHIPS + z, me)
    z_next = (y * Z_CHIPS + (z + 1) % Z_CHIPS, me)
    z_prev = (y * Z_CHIPS + (z + Z_CHIPS - 1) % Z_CHIPS, me)
    partner = (row, 2 * x + 1 - core)
    peers = [(row, (me + d) % n_col) for d in range(1, n_col)]

    barrier = pltpu.get_barrier_semaphore()
    greeted = peers + [y_next, y_prev, z_next, z_prev]
    for other in greeted:
        pl.semaphore_signal(barrier, inc=1, device_id=other, device_id_type=MESH)
    pl.semaphore_wait(barrier, len(greeted))

    started = []

    def send(slot, src, dst, target):
        copy = pltpu.make_async_remote_copy(
            src_ref=src,
            dst_ref=dst,
            send_sem=send_sem.at[slot],
            recv_sem=recv_sem.at[slot],
            device_id=target,
            device_id_type=MESH,
        )
        copy.start()
        started.append(copy)
        return copy

    rows_piece = stored // COLORS
    rows_half = rows_piece // 2

    def span(dx, shade, half=None):
        start = (2 * chip(dx) + core) * stored + shade * rows_piece
        size = rows_piece
        if half is not None:
            start, size = start + half * rows_half, rows_half
        return y_buf.at[pl.ds(pl.multiple_of(start, 16), size), :]

    own_piece = items_ref.at[pl.ds(pl.multiple_of(color * rows_piece, 16), rows_piece), :]
    own_rows = y_buf.at[pl.ds(pl.multiple_of(me * stored, 16), stored), :]
    from_left = send(1, own_piece, span(0, color), on_x(1))
    from_right = send(2, own_piece, span(0, color), on_x(3))
    own_conf = conf_buf.at[pl.ds(me * n_blocks, n_blocks)]
    conf_in = []
    for d, other in enumerate(peers):
        src = conf_ref.at[:, pl.ds(pl.multiple_of(other[1] * part, 16), part), :]
        conf_in.append(send(29 + d, src, own_conf, other))
    core_in = [send(0, items_ref, own_rows, partner)]

    locals_ = [
        pltpu.make_async_copy(items_ref, own_rows, local_sem.at[0]),
        pltpu.make_async_copy(
            conf_ref.at[:, pl.ds(pl.multiple_of(me * part, 16), part), :],
            own_conf,
            local_sem.at[1],
        ),
    ]
    for half in range(2):
        locals_.append(
            pltpu.make_async_copy(
                users_ref.at[pl.ds(pl.multiple_of(half * tile + me * part, 16), part), :],
                mine.at[pl.ds(half * part, part), :],
                local_sem.at[2 + half],
            )
        )
    for copy in locals_:
        copy.start()

    lane = lax.broadcasted_iota(jnp.int32, (1, 128), 1)
    upper = (lane >= all_blocks).astype(jnp.int32)
    block_of = lane - upper * all_blocks

    def rank_step(b, carry):
        count, table = carry
        hit = (owner_ref[b] == me).astype(jnp.int32)
        table = jnp.where(block_of == b, hit * (count + 1) - 1, table)
        return count + hit, table

    count, table = lax.fori_loop(
        0, all_blocks, rank_step, (jnp.int32(0), jnp.full((1, 128), -1, jnp.int32))
    )
    count = jnp.maximum(count, 1)

    def pick_step(n, carry):
        wanted = lax.rem(cols_ref[n], count)
        hit = (table == wanted) & (upper == rows_ref[n])
        pick_buf[pl.ds(me * n_blocks + n, 1), :] = hit.astype(F32)
        return carry

    lax.fori_loop(0, n_blocks, pick_step, 0)
    own_pick = pick_buf.at[pl.ds(pl.multiple_of(me * n_blocks, 8), n_blocks), :]
    pick_in = [send(36 + d, own_pick, own_pick, other) for d, other in enumerate(peers)]

    yz_in = []

    def spread(index, dx):
        base = 5 + 4 * index
        yz_in.append(
            [
                send(base, span(dx, color), span(dx, color), y_next),
                send(base + 1, span(dx, color), span(dx, color), y_prev),
                send(base + 2, span(dx, color, 0), span(dx, color, 0), z_next),
                send(base + 3, span(dx, color, 1), span(dx, color, 1), z_prev),
            ]
        )

    def to_partner(index, which, dx, shade):
        piece = span(dx, shade)
        core_in.append(send(17 + 4 * index + which, piece, piece, partner))

    from_left.wait_recv()
    far_first = send(3, span(3, color, 0), span(3, color, 0), on_x(1))
    spread(0, 3)
    from_right.wait_recv()
    far_second = send(4, span(1, color, 1), span(1, color, 1), on_x(3))
    spread(1, 1)
    to_partner(0, 0, 3, color)
    to_partner(1, 0, 1, color)
    far_first.wait_recv()
    far_second.wait_recv()
    spread(2, 2)
    to_partner(2, 0, 2, color)

    for index, dx in ((0, 3), (1, 1), (2, 2)):
        below, above, low, high = yz_in[index]
        below.wait_recv()
        to_partner(index, 1, dx, (color + 3) % COLORS)
        above.wait_recv()
        to_partner(index, 2, dx, (color + 1) % COLORS)
        low.wait_recv()
        high.wait_recv()
        to_partner(index, 3, dx, (color + 2) % COLORS)

    for copy in locals_:
        copy.wait()
    for copy in conf_in + pick_in:
        copy.wait_recv()

    def widen(n, carry):
        start = pl.multiple_of(n * part, 16)
        wide[pl.ds(start, part), :] = conf_buf[n].astype(F32)
        return carry

    lax.fori_loop(0, total, widen, 0, unroll=8)
    picks = pick_buf[...].T[: 2 * all_blocks].astype(BF16)
    for u in range(part):
        weights = wide[pl.ds(u, total, stride=part), :]
        preference = jnp.where(weights > 0, 1.0 + weights, 0.0)
        both = jnp.concatenate([weights, preference], axis=1).astype(BF16)
        sums = jnp.dot(picks, both, preferred_element_type=F32)
        for half in range(2):
            place = pl.ds(half * part + u, all_blocks, stride=users)
            band = sums[half * all_blocks : (half + 1) * all_blocks]
            c_buf[place, :] = band[:, :tile]
            p_buf[place, :] = band[:, tile:]

    for copy in core_in:
        copy.wait_recv()

    step_blocks = 4
    chunk = step_blocks * tile

    def sweep(values, first):
        high = values.astype(BF16)
        low = (values - high.astype(F32)).astype(BF16)
        left = jnp.concatenate([high, low], axis=0)

        def body(i, acc):
            factors = y_buf[pl.ds(pl.multiple_of(i * chunk, chunk), chunk), :]
            products = lax.dot_general(
                left, factors, (((1,), (1,)), ((), ())), preferred_element_type=F32
            )
            scores = products[:users]
            plain = scores + products[users:]

            def lanes(ref):
                return jnp.concatenate(
                    [
                        ref[pl.ds(pl.multiple_of((i * step_blocks + j) * users, users), users), :]
                        for j in range(step_blocks)
                    ],
                    axis=1,
                )

            inner = (scores * lanes(c_buf)).astype(BF16).astype(F32) + plain
            if first:
                inner = lanes(p_buf) - inner
            top = inner.astype(BF16)
            rest = (inner - top.astype(F32)).astype(BF16)
            return acc + jnp.dot(
                jnp.concatenate([top, rest], axis=0), factors, preferred_element_type=F32
            )

        acc = lax.fori_loop(
            0, n_items // chunk, body, jnp.zeros((2 * users, width), F32), unroll=2
        )
        return acc[:users] + acc[users:]

    answer = mine[...]
    residual = sweep(answer, True) - regular * answer
    direction = residual
    squares = jnp.sum(residual * residual, axis=1, keepdims=True)
    for step in range(CG_STEPS):
        image = sweep(direction, False) + regular * direction
        step_size = squares / (jnp.sum(direction * image, axis=1, keepdims=True) + epsilon)
        answer = answer + step_size * direction
        if step + 1 < CG_STEPS:
            residual = residual - step_size * image
            fresh = jnp.sum(residual * residual, axis=1, keepdims=True)
            direction = residual + (fresh / (squares + epsilon)) * direction
            squares = fresh

    for half in range(2):
        result[half] = answer[half * part : (half + 1) * part]
    own_out = out_ref.at[:, pl.ds(pl.multiple_of(me * part, 16), part), :]
    out_in = [send(43 + d, result, own_out, other) for d, other in enumerate(peers)]
    keep = pltpu.make_async_copy(result, own_out, local_sem.at[4])
    keep.start()
    keep.wait()
    for copy in out_in:
        copy.wait_recv()
    for copy in started:
        copy.wait_send()


def local(confidences, block_rows, block_cols, item_owner, item_factors, user_factors):
    n_blocks, tile = confidences.shape[:2]
    stored, width = item_factors.shape
    all_blocks = item_owner.shape[0]
    n_items = all_blocks * tile
    n_col = n_items // stored
    part = tile // n_col
    total = n_blocks * n_col
    users = 2 * part
    slots = 50
    any_spec = pl.BlockSpec(memory_space=pl.ANY)
    smem = pl.BlockSpec(memory_space=pltpu.SMEM)
    out = pl.pallas_call(
        kernel,
        out_shape=jax.ShapeDtypeStruct((2, tile, width), F32),
        in_specs=[any_spec, smem, smem, smem, any_spec, any_spec],
        out_specs=any_spec,
        scratch_shapes=[
            pltpu.VMEM((n_items, width), BF16),
            pltpu.VMEM((total, part, tile), BF16),
            pltpu.VMEM((total, 128), F32),
            pltpu.VMEM((total * part, tile), F32),
            pltpu.VMEM((all_blocks * users, tile), F32),
            pltpu.VMEM((all_blocks * users, tile), F32),
            pltpu.VMEM((users, width), F32),
            pltpu.VMEM((2, part, width), F32),
            pltpu.SemaphoreType.DMA((5,)),
            pltpu.SemaphoreType.DMA((slots,)),
            pltpu.SemaphoreType.DMA((slots,)),
        ],
        compiler_params=pltpu.CompilerParams(
            collective_id=0, has_side_effects=True, vmem_limit_bytes=40 * 1024 * 1024
        ),
    )(confidences, block_rows, block_cols, item_owner, item_factors, user_factors)
    return out.reshape(user_factors.shape)


def solution(mesh):
    in_specs = (
        P(("row", "col"), None, None),
        P(("row", "col")),
        P(("row", "col")),
        P(),
        P("col", None),
        P("row", None),
    )
    out_specs = P("row", None)
    return jax.shard_map(local, mesh=mesh, in_specs=in_specs, out_specs=out_specs, check_vma=False)
```

time: 833 us -> 65.3 us (0.08)
  waiting for transfers between devices: 744 us -> 0 us
  Pallas kernels: 0 us -> 59.3 us
  matrix products: 49.7 us -> 0 us
  between operations: 16.5 us -> 0.02 us
  local copies, waits for them, and re-layouts: 14.2 us -> 5.75 us
    psum x5 -> x0, waiting for transfers between devices: 707 us -> none  [the longest x1 409 us: local(): gram_matrix = lax.psum(local_gram, ('row', 'col'))]
    pallas_call x0 -> x1, Pallas kernels: none -> 59.3 us  [local(): pl.pallas_call(kernel, out_shape=jax.ShapeDtypeStruct((2, tile, width), F...]
    dot_general x15 -> x0, matrix products: 49.7 us -> none  [the longest x5 21.7 us: segment_total(): jnp.einsum('nb,nuk->buk', onehot, contrib, precision=lax.Precision.HIGHEST)]
    all_gather x1 -> x0, waiting for transfers between devices: 35.6 us -> none  [local(): lax.all_gather(item_factors, 'col', axis=0, tiled=True)]
    gather x5 -> x0, local copies, waits for them, and re-layouts: 11.2 us -> none  [the longest x4 7.42 us: block_term(): jnp.take(rounded.reshape(slab_blocks, tile, widths), block_rows, axis=0)]
  transfers between devices with their start and end apart: 6 -> 0, of which waited for: 6 -> 0; matrix products, arithmetic and copies ran while one was open for 4% -> 0% of each run, Pallas kernels for 0% -> 0%
where the time goes in v1:
time: 65.3 us; the launch traced here: 65.1 us
  Pallas kernels  59.3 us (91%)
  local copies, waits for them, and re-layouts  5.75 us (9%)
    pallas_call x1, Pallas kernels, local(): pl.pallas_call(kernel, out_shape=jax.ShapeDtypeStruct((2, tile, width), F...  59.3 us
    unnamed x13, local copies, waits for them, and re-layouts  5.75 us

profile of v1, /device:TPU:1, one launch (start us, length us, event | category | flops | bytes accessed | tf_op | source)
XLA Modules:
  0.0 65.1 jit_solution(5067083141218693491)
XLA Ops:
  0.0 0.0 copy-start
  0.0 1.1 %copy-done = bf16[24,128,128]{2,1,0:T(8,128)(2,1)S(1)} copy-done((bf16[24,128,128]{2,1,0:T(8,128)(2,1)S(1)}, bf16[24,128,128]{2,1,0:T(8,128)(2,1)}, u32[]{:S(2)}) %copy-start) | copy-done | bytes 786456
  1.1 0.0 copy-start.1
  1.1 1.0 %copy-done.1 = bf16[768,256]{1,0:T(8,128)(2,1)S(1)} copy-done((bf16[768,256]{1,0:T(8,128)(2,1)S(1)}, bf16[768,256]{1,0:T(8,128)(2,1)}, u32[]{:S(2)}) %copy-start.1) | copy-done | bytes 393240
  2.1 0.0 copy-start.2
  2.1 0.9 %copy-done.2 = f32[256,256]{1,0:T(8,128)S(1)} copy-done((f32[256,256]{1,0:T(8,128)S(1)}, f32[256,256]{1,0:T(8,128)}, u32[]{:S(2)}) %copy-start.2) | copy-done | bytes 262168
  3.1 0.0 copy-start.3
  3.1 0.7 %copy-done.3 = s32[24]{0:T(128)S(1)} copy-done((s32[24]{0:T(128)S(1)}, s32[24]{0:T(128)}, u32[]{:S(2)}) %copy-start.3) | copy-done | bytes 120
  3.7 0.0 copy-start.4
  3.7 0.7 %copy-done.4 = s32[24]{0:T(128)S(1)} copy-done((s32[24]{0:T(128)S(1)}, s32[24]{0:T(128)}, u32[]{:S(2)}) %copy-start.4) | copy-done | bytes 120
  4.4 0.0 copy-start.5
  4.4 0.7 %copy-done.5 = s32[48]{0:T(128)S(1)} copy-done((s32[48]{0:T(128)S(1)}, s32[48]{0:T(128)}, u32[]{:S(2)}) %copy-start.5) | copy-done | bytes 216
  5.0 59.3 %shard_map.64 = f32[2,128,256]{2,1,0:T(8,128)S(1)} custom-call(bf16[24,128,128]{2,1,0:T(8,128)(2,1)S(1)} %copy-done, s32[24]{0:T(128)S(1)} %copy-done.3, s32[24]{0:T(128)S(1)} %copy-done.4, s32[48]{0:T(128)S(1)} %copy-done.5, bf16[768,256]{1,0:T(8,128)(2,1)S(1)} %copy-done.1, f32[256,256]{1,0:T(8,128)S(1)} %copy-done.2), custom_call_target="tpu_custom_call" | custom-call | tf_op jit(solution)/shard_map/pallas_call | solution.py:300
  64.4 0.7 %copy.8 = f32[256,256]{1,0:T(8,128)} copy(f32[256,256]{1,0:T(8,128)S(1)} %bitcast.1) | data formatting | bytes 524288
Async XLA Ops:
  0.0 1.1 %copy-start = (bf16[24,128,128]{2,1,0:T(8,128)(2,1)S(1)}, bf16[24,128,128]{2,1,0:T(8,128)(2,1)}, u32[]{:S(2)}) copy-start(bf16[24,128,128]{2,1,0:T(8,128)(2,1)} %conf_ref.1) | copy-start | bytes 2359300
  1.1 1.0 %copy-start.1 = (bf16[768,256]{1,0:T(8,128)(2,1)S(1)}, bf16[768,256]{1,0:T(8,128)(2,1)}, u32[]{:S(2)}) copy-start(bf16[768,256]{1,0:T(8,128)(2,1)} %items_ref.1) | copy-start | bytes 1179652
  2.1 0.9 %copy-start.2 = (f32[256,256]{1,0:T(8,128)S(1)}, f32[256,256]{1,0:T(8,128)}, u32[]{:S(2)}) copy-start(f32[256,256]{1,0:T(8,128)} %users_ref.1) | copy-start | bytes 786436
  3.1 0.7 %copy-start.3 = (s32[24]{0:T(128)S(1)}, s32[24]{0:T(128)}, u32[]{:S(2)}) copy-start(s32[24]{0:T(128)} %rows_ref.1) | copy-start | bytes 292
  3.7 0.7 %copy-start.4 = (s32[24]{0:T(128)S(1)}, s32[24]{0:T(128)}, u32[]{:S(2)}) copy-start(s32[24]{0:T(128)} %cols_ref.1) | copy-start | bytes 292
  4.4 0.7 %copy-start.5 = (s32[48]{0:T(128)S(1)}, s32[48]{0:T(128)}, u32[]{:S(2)}) copy-start(s32[48]{0:T(128)} %owner_ref.1) | copy-start | bytes 580

commit v2 on v1

--- a/solution.py
+++ b/solution.py
@@ -21,13 +21,14 @@
 
 def kernel(
     conf_ref,
-    rows_ref,
-    cols_ref,
-    owner_ref,
+    rows_hbm,
+    cols_hbm,
+    owner_hbm,
     items_ref,
     users_ref,
     out_ref,
     y_buf,
+    yt_buf,
     conf_buf,
     pick_buf,
     wide,
@@ -35,6 +36,9 @@
     p_buf,
     mine,
     result,
+    rows_ref,
+    cols_ref,
+    owner_ref,
     local_sem,
     send_sem,
     recv_sem,
@@ -42,7 +46,7 @@
     n_blocks, tile = conf_ref.shape[0], conf_ref.shape[2]
     stored = items_ref.shape[0]
     n_items, width = y_buf.shape
-    all_blocks = owner_ref.shape[0]
+    all_blocks = owner_hbm.shape[0]
     n_col = n_items // stored
     part = tile // n_col
     total = n_blocks * n_col
@@ -65,7 +69,15 @@
     z_next = (y * Z_CHIPS + (z + 1) % Z_CHIPS, me)
     z_prev = (y * Z_CHIPS + (z + Z_CHIPS - 1) % Z_CHIPS, me)
     partner = (row, 2 * x + 1 - core)
-    peers = [(row, (me + d) % n_col) for d in range(1, n_col)]
+    peers = [(row, 2 * chip(d // 2) + (core + d) % 2) for d in range(1, n_col)]
+
+    ids_in = [
+        pltpu.make_async_copy(rows_hbm, rows_ref, local_sem.at[5]),
+        pltpu.make_async_copy(cols_hbm, cols_ref, local_sem.at[6]),
+        pltpu.make_async_copy(owner_hbm, owner_ref, local_sem.at[7]),
+    ]
+    for copy in ids_in:
+        copy.start()
 
     barrier = pltpu.get_barrier_semaphore()
     greeted = peers + [y_next, y_prev, z_next, z_prev]
@@ -103,10 +115,15 @@
     from_left = send(1, own_piece, span(0, color), on_x(1))
     from_right = send(2, own_piece, span(0, color), on_x(3))
     own_conf = conf_buf.at[pl.ds(me * n_blocks, n_blocks)]
-    conf_in = []
-    for d, other in enumerate(peers):
-        src = conf_ref.at[:, pl.ds(pl.multiple_of(other[1] * part, 16), part), :]
-        conf_in.append(send(29 + d, src, own_conf, other))
+    conf_in = {}
+
+    def send_conf(*offsets):
+        for d in offsets:
+            other = peers[d - 1]
+            src = conf_ref.at[:, pl.ds(pl.multiple_of(other[1] * part, 16), part), :]
+            conf_in[d] = send(28 + d, src, own_conf, other)
+
+    send_conf(1)
     core_in = [send(0, items_ref, own_rows, partner)]
 
     locals_ = [
@@ -128,6 +145,9 @@
     for copy in locals_:
         copy.start()
 
+    for copy in ids_in:
+        copy.wait()
+
     lane = lax.broadcasted_iota(jnp.int32, (1, 128), 1)
     upper = (lane >= all_blocks).astype(jnp.int32)
     block_of = lane - upper * all_blocks
@@ -172,10 +192,11 @@
 
     from_left.wait_recv()
     far_first = send(3, span(3, color, 0), span(3, color, 0), on_x(1))
-    spread(0, 3)
     from_right.wait_recv()
     far_second = send(4, span(1, color, 1), span(1, color, 1), on_x(3))
+    spread(0, 3)
     spread(1, 1)
+    send_conf(2, 3, 6, 7, 4, 5)
     to_partner(0, 0, 3, color)
     to_partner(1, 0, 1, color)
     far_first.wait_recv()
@@ -195,17 +216,21 @@
 
     for copy in locals_:
         copy.wait()
-    for copy in conf_in + pick_in:
+    for copy in core_in + pick_in + list(conf_in.values()):
         copy.wait_recv()
 
-    def widen(n, carry):
-        start = pl.multiple_of(n * part, 16)
-        wide[pl.ds(start, part), :] = conf_buf[n].astype(F32)
+    def widen(block, carry):
+        wide[pl.ds(pl.multiple_of(block * part, 16), part), :] = conf_buf[block].astype(F32)
         return carry
 
     lax.fori_loop(0, total, widen, 0, unroll=8)
+    for shard in range(n_col):
+        rows_of = slice(shard * stored, (shard + 1) * stored)
+        yt_buf[:, rows_of] = y_buf[rows_of, :].T
+
     picks = pick_buf[...].T[: 2 * all_blocks].astype(BF16)
-    for u in range(part):
+
+    def gather(u, carry):
         weights = wide[pl.ds(u, total, stride=part), :]
         preference = jnp.where(weights > 0, 1.0 + weights, 0.0)
         both = jnp.concatenate([weights, preference], axis=1).astype(BF16)
@@ -215,9 +240,9 @@
             band = sums[half * all_blocks : (half + 1) * all_blocks]
             c_buf[place, :] = band[:, :tile]
             p_buf[place, :] = band[:, tile:]
-
-    for copy in core_in:
-        copy.wait_recv()
+        return carry
+
+    lax.fori_loop(0, part, gather, 0, unroll=4)
 
     step_blocks = 4
     chunk = step_blocks * tile
@@ -226,54 +251,56 @@
         high = values.astype(BF16)
         low = (values - high.astype(F32)).astype(BF16)
         left = jnp.concatenate([high, low], axis=0)
-
-        def body(i, acc):
-            factors = y_buf[pl.ds(pl.multiple_of(i * chunk, chunk), chunk), :]
-            products = lax.dot_general(
-                left, factors, (((1,), (1,)), ((), ())), preferred_element_type=F32
-            )
+        acc = jnp.zeros((2 * users, width), F32)
+        for i in range(n_items // chunk):
+            columns = pl.ds(i * chunk, chunk)
+            products = jnp.dot(left, yt_buf[:, columns], preferred_element_type=F32)
             scores = products[:users]
             plain = scores + products[users:]
 
             def lanes(ref):
                 return jnp.concatenate(
-                    [
-                        ref[pl.ds(pl.multiple_of((i * step_blocks + j) * users, users), users), :]
-                        for j in range(step_blocks)
-                    ],
+                    [ref[pl.ds((i * step_blocks + j) * users, users), :] for j in range(step_blocks)],
                     axis=1,
                 )
 
             inner = (scores * lanes(c_buf)).astype(BF16).astype(F32) + plain
-            if first:
-                inner = lanes(p_buf) - inner
+            inner = jnp.where(first, lanes(p_buf) - inner, inner)
             top = inner.astype(BF16)
             rest = (inner - top.astype(F32)).astype(BF16)
-            return acc + jnp.dot(
-                jnp.concatenate([top, rest], axis=0), factors, preferred_element_type=F32
+            acc = acc + jnp.dot(
+                jnp.concatenate([top, rest], axis=0),
+                y_buf[columns, :],
+                preferred_element_type=F32,
             )
-
-        acc = lax.fori_loop(
-            0, n_items // chunk, body, jnp.zeros((2 * users, width), F32), unroll=2
+        return acc[:users] + acc[users:]
+
+    def step(i, carry):
+        answer, residual, direction, squares = carry
+        first = i == 0
+        image = sweep(direction, first)
+        start = image - regular * direction
+        start_squares = jnp.sum(start * start, axis=1, keepdims=True)
+        image = image + regular * direction
+        step_size = squares / (jnp.sum(direction * image, axis=1, keepdims=True) + epsilon)
+        moved = answer + step_size * direction
+        later = residual - step_size * image
+        fresh = jnp.sum(later * later, axis=1, keepdims=True)
+        turned = later + (fresh / (squares + epsilon)) * direction
+        return (
+            jnp.where(first, answer, moved),
+            jnp.where(first, start, later),
+            jnp.where(first, start, turned),
+            jnp.where(first, start_squares, fresh),
         )
-        return acc[:users] + acc[users:]
-
-    answer = mine[...]
-    residual = sweep(answer, True) - regular * answer
-    direction = residual
-    squares = jnp.sum(residual * residual, axis=1, keepdims=True)
-    for step in range(CG_STEPS):
-        image = sweep(direction, False) + regular * direction
-        step_size = squares / (jnp.sum(direction * image, axis=1, keepdims=True) + epsilon)
-        answer = answer + step_size * direction
-        if step + 1 < CG_STEPS:
-            residual = residual - step_size * image
-            fresh = jnp.sum(residual * residual, axis=1, keepdims=True)
-            direction = residual + (fresh / (squares + epsilon)) * direction
-            squares = fresh
+
+    guess = mine[...]
+    answer = lax.fori_loop(
+        0, CG_STEPS + 1, step, (guess, guess, guess, jnp.ones((users, 1), F32))
+    )[0]
 
     for half in range(2):
-        result[half] = answer[half * part : (half + 1) * part]
+        result[half] = answer[half * part : (half + 1) * part].astype(BF16)
     own_out = out_ref.at[:, pl.ds(pl.multiple_of(me * part, 16), part), :]
     out_in = [send(43 + d, result, own_out, other) for d, other in enumerate(peers)]
     keep = pltpu.make_async_copy(result, own_out, local_sem.at[4])
@@ -295,31 +322,34 @@
     total = n_blocks * n_col
     users = 2 * part
     slots = 50
-    any_spec = pl.BlockSpec(memory_space=pl.ANY)
-    smem = pl.BlockSpec(memory_space=pltpu.SMEM)
+    hbm = pl.BlockSpec(memory_space=pltpu.HBM)
     out = pl.pallas_call(
         kernel,
-        out_shape=jax.ShapeDtypeStruct((2, tile, width), F32),
-        in_specs=[any_spec, smem, smem, smem, any_spec, any_spec],
-        out_specs=any_spec,
+        out_shape=jax.ShapeDtypeStruct((2, tile, width), BF16),
+        in_specs=[hbm] * 6,
+        out_specs=hbm,
         scratch_shapes=[
             pltpu.VMEM((n_items, width), BF16),
+            pltpu.VMEM((width, n_items), BF16),
             pltpu.VMEM((total, part, tile), BF16),
             pltpu.VMEM((total, 128), F32),
             pltpu.VMEM((total * part, tile), F32),
             pltpu.VMEM((all_blocks * users, tile), F32),
             pltpu.VMEM((all_blocks * users, tile), F32),
             pltpu.VMEM((users, width), F32),
-            pltpu.VMEM((2, part, width), F32),
-            pltpu.SemaphoreType.DMA((5,)),
+            pltpu.VMEM((2, part, width), BF16),
+            pltpu.SMEM((n_blocks,), jnp.int32),
+            pltpu.SMEM((n_blocks,), jnp.int32),
+            pltpu.SMEM((all_blocks,), jnp.int32),
+            pltpu.SemaphoreType.DMA((8,)),
             pltpu.SemaphoreType.DMA((slots,)),
             pltpu.SemaphoreType.DMA((slots,)),
         ],
         compiler_params=pltpu.CompilerParams(
-            collective_id=0, has_side_effects=True, vmem_limit_bytes=40 * 1024 * 1024
+            collective_id=0, has_side_effects=True, vmem_limit_bytes=64 * 1024 * 1024
         ),
     )(confidences, block_rows, block_cols, item_owner, item_factors, user_factors)
-    return out.reshape(user_factors.shape)
+    return out.reshape(user_factors.shape).astype(user_factors.dtype)
 
 
 def solution(mesh):

time: 65.3 us -> 47.2 us (0.72)
  Pallas kernels: 59.3 us -> 45.5 us
  local copies, waits for them, and re-layouts: 5.75 us -> 0 us
  other arithmetic: 0 us -> 1.63 us
    pallas_call x1, Pallas kernels: 59.3 us -> 45.5 us  [local(): pl.pallas_call(kernel, out_shape=jax.ShapeDtypeStruct((2, tile, width), B...]
    unnamed x13 -> x0, local copies, waits for them, and re-layouts: 5.75 us -> none
    convert_element_type x0 -> x1, other arithmetic: none -> 1.63 us  [local(): return out.reshape(user_factors.shape).astype(user_factors.dtype)]
where the time goes in v2:
time: 47.2 us; the launch traced here: 47.1 us
  Pallas kernels  45.5 us (96%)
  other arithmetic  1.63 us (3%)
    pallas_call x1, Pallas kernels, local(): pl.pallas_call(kernel, out_shape=jax.ShapeDtypeStruct((2, tile, width), B...  45.5 us
    convert_element_type x1, other arithmetic, local(): return out.reshape(user_factors.shape).astype(user_factors.dtype)  1.63 us

profile of v2, /device:TPU:1, one launch (start us, length us, event | category | flops | bytes accessed | tf_op | source)
XLA Modules:
  0.0 47.1 jit_solution(6926511296982094640)
XLA Ops:
  0.0 45.5 %shard_map.64 = bf16[2,128,256]{2,1,0:T(8,128)(2,1)} custom-call(bf16[24,128,128]{2,1,0:T(8,128)(2,1)} %conf_ref.1, s32[24]{0:T(128)} %rows_hbm.1, s32[24]{0:T(128)} %cols_hbm.1, s32[48]{0:T(128)} %owner_hbm.1, bf16[768,256]{1,0:T(8,128)(2,1)} %items_ref.1, f32[256,256]{1,0:T(8,128)} %users_ref.1), custom_call_target="tpu_custom_call" | custom-call | tf_op jit(solution)/shard_map/pallas_call | solution.py:326
  45.5 1.6 %bitcast_convert_fusion = f32[256,256]{1,0:T(8,128)} fusion(bf16[2,128,256]{2,1,0:T(8,128)(2,1)} %shard_map.64), kind=kLoop, calls=%fused_computation | loop fusion | flops 65536 | bytes 393216 | tf_op jit(solution)/shard_map/convert_element_type | solution.py:352

commit v3 on v2

--- a/solution.py
+++ b/solution.py
@@ -110,10 +110,15 @@
             start, size = start + half * rows_half, rows_half
         return y_buf.at[pl.ds(pl.multiple_of(start, 16), size), :]
 
-    own_piece = items_ref.at[pl.ds(pl.multiple_of(color * rows_piece, 16), rows_piece), :]
+    def own_half(half):
+        start = color * rows_piece + half * rows_half
+        return items_ref.at[pl.ds(pl.multiple_of(start, 16), rows_half), :]
+
     own_rows = y_buf.at[pl.ds(pl.multiple_of(me * stored, 16), stored), :]
-    from_left = send(1, own_piece, span(0, color), on_x(1))
-    from_right = send(2, own_piece, span(0, color), on_x(3))
+    left_0 = send(1, own_half(0), span(0, color, 0), on_x(1))
+    right_1 = send(2, own_half(1), span(0, color, 1), on_x(3))
+    left_1 = send(3, own_half(1), span(0, color, 1), on_x(1))
+    right_0 = send(4, own_half(0), span(0, color, 0), on_x(3))
     own_conf = conf_buf.at[pl.ds(me * n_blocks, n_blocks)]
     conf_in = {}
 
@@ -121,7 +126,7 @@
         for d in offsets:
             other = peers[d - 1]
             src = conf_ref.at[:, pl.ds(pl.multiple_of(other[1] * part, 16), part), :]
-            conf_in[d] = send(28 + d, src, own_conf, other)
+            conf_in[d] = send(37 + d, src, own_conf, other)
 
     send_conf(1)
     core_in = [send(0, items_ref, own_rows, partner)]
@@ -171,47 +176,51 @@
 
     lax.fori_loop(0, n_blocks, pick_step, 0)
     own_pick = pick_buf.at[pl.ds(pl.multiple_of(me * n_blocks, 8), n_blocks), :]
-    pick_in = [send(36 + d, own_pick, own_pick, other) for d, other in enumerate(peers)]
-
-    yz_in = []
-
-    def spread(index, dx):
-        base = 5 + 4 * index
-        yz_in.append(
-            [
-                send(base, span(dx, color), span(dx, color), y_next),
-                send(base + 1, span(dx, color), span(dx, color), y_prev),
-                send(base + 2, span(dx, color, 0), span(dx, color, 0), z_next),
-                send(base + 3, span(dx, color, 1), span(dx, color, 1), z_prev),
-            ]
-        )
+    pick_in = [send(45 + d, own_pick, own_pick, other) for d, other in enumerate(peers)]
+
+    yz_in = {}
+
+    def spread(index, dx, half):
+        base = 8 + 6 * index + 3 * half
+        piece = span(dx, color, half)
+        yz_in[index, half] = [
+            send(base, piece, piece, y_next),
+            send(base + 1, piece, piece, y_prev),
+            send(base + 2, piece, piece, z_prev if half else z_next),
+        ]
 
     def to_partner(index, which, dx, shade):
         piece = span(dx, shade)
-        core_in.append(send(17 + 4 * index + which, piece, piece, partner))
-
-    from_left.wait_recv()
-    far_first = send(3, span(3, color, 0), span(3, color, 0), on_x(1))
-    from_right.wait_recv()
-    far_second = send(4, span(1, color, 1), span(1, color, 1), on_x(3))
-    spread(0, 3)
-    spread(1, 1)
+        core_in.append(send(26 + 4 * index + which, piece, piece, partner))
+
+    left_0.wait_recv()
+    far_0 = send(5, span(3, color, 0), span(3, color, 0), on_x(1))
+    spread(0, 3, 0)
+    right_1.wait_recv()
+    far_1 = send(6, span(1, color, 1), span(1, color, 1), on_x(3))
+    spread(1, 1, 1)
     send_conf(2, 3, 6, 7, 4, 5)
+    left_1.wait_recv()
+    spread(0, 3, 1)
+    right_0.wait_recv()
+    spread(1, 1, 0)
     to_partner(0, 0, 3, color)
     to_partner(1, 0, 1, color)
-    far_first.wait_recv()
-    far_second.wait_recv()
-    spread(2, 2)
+    far_0.wait_recv()
+    spread(2, 2, 0)
+    far_1.wait_recv()
+    spread(2, 2, 1)
     to_partner(2, 0, 2, color)
 
     for index, dx in ((0, 3), (1, 1), (2, 2)):
-        below, above, low, high = yz_in[index]
-        below.wait_recv()
+        for half in range(2):
+            yz_in[index, half][0].wait_recv()
         to_partner(index, 1, dx, (color + 3) % COLORS)
-        above.wait_recv()
+        for half in range(2):
+            yz_in[index, half][1].wait_recv()
         to_partner(index, 2, dx, (color + 1) % COLORS)
-        low.wait_recv()
-        high.wait_recv()
+        for half in range(2):
+            yz_in[index, half][2].wait_recv()
         to_partner(index, 3, dx, (color + 2) % COLORS)
 
     for copy in locals_:
@@ -244,7 +253,7 @@
 
     lax.fori_loop(0, part, gather, 0, unroll=4)
 
-    step_blocks = 4
+    step_blocks = 2
     chunk = step_blocks * tile
 
     def sweep(values, first):
@@ -302,7 +311,7 @@
     for half in range(2):
         result[half] = answer[half * part : (half + 1) * part].astype(BF16)
     own_out = out_ref.at[:, pl.ds(pl.multiple_of(me * part, 16), part), :]
-    out_in = [send(43 + d, result, own_out, other) for d, other in enumerate(peers)]
+    out_in = [send(52 + d, result, own_out, other) for d, other in enumerate(peers)]
     keep = pltpu.make_async_copy(result, own_out, local_sem.at[4])
     keep.start()
     keep.wait()
@@ -321,7 +330,7 @@
     part = tile // n_col
     total = n_blocks * n_col
     users = 2 * part
-    slots = 50
+    slots = 59
     hbm = pl.BlockSpec(memory_space=pltpu.HBM)
     out = pl.pallas_call(
         kernel,

time: 47.2 us -> 46.2 us (0.979)
  Pallas kernels: 45.5 us -> 44.4 us
    pallas_call x1, Pallas kernels: 45.5 us -> 44.4 us  [local(): pl.pallas_call(kernel, out_shape=jax.ShapeDtypeStruct((2, tile, width), B...]
where the time goes in v3:
time: 46.2 us; the launch traced here: 46.1 us
  Pallas kernels  44.4 us (96%)
  other arithmetic  1.63 us (4%)
    pallas_call x1, Pallas kernels, local(): pl.pallas_call(kernel, out_shape=jax.ShapeDtypeStruct((2, tile, width), B...  44.4 us
    convert_element_type x1, other arithmetic, local(): return out.reshape(user_factors.shape).astype(user_factors.dtype)  1.63 us

profile of v3, /device:TPU:1, one launch (start us, length us, event | category | flops | bytes accessed | tf_op | source)
XLA Modules:
  0.0 46.1 jit_solution(9011222113557990021)
XLA Ops:
  0.0 44.4 %shard_map.64 = bf16[2,128,256]{2,1,0:T(8,128)(2,1)} custom-call(bf16[24,128,128]{2,1,0:T(8,128)(2,1)} %conf_ref.1, s32[24]{0:T(128)} %rows_hbm.1, s32[24]{0:T(128)} %cols_hbm.1, s32[48]{0:T(128)} %owner_hbm.1, bf16[768,256]{1,0:T(8,128)(2,1)} %items_ref.1, f32[256,256]{1,0:T(8,128)} %users_ref.1), custom_call_target="tpu_custom_call" | custom-call | tf_op jit(solution)/shard_map/pallas_call | solution.py:335
  44.4 1.6 %bitcast_convert_fusion = f32[256,256]{1,0:T(8,128)} fusion(bf16[2,128,256]{2,1,0:T(8,128)(2,1)} %shard_map.64), kind=kLoop, calls=%fused_computation | loop fusion | flops 65536 | bytes 393216 | tf_op jit(solution)/shard_map/convert_element_type | solution.py:361

commit v4 on v3

--- a/solution.py
+++ b/solution.py
@@ -66,8 +66,7 @@
 
     y_next = (((y + 1) % Y_CHIPS) * Z_CHIPS + z, me)
     y_prev = (((y + Y_CHIPS - 1) % Y_CHIPS) * Z_CHIPS + z, me)
-    z_next = (y * Z_CHIPS + (z + 1) % Z_CHIPS, me)
-    z_prev = (y * Z_CHIPS + (z + Z_CHIPS - 1) % Z_CHIPS, me)
+    z_pair = (y * Z_CHIPS + z + 1 - 2 * (z % 2), me)
     partner = (row, 2 * x + 1 - core)
     peers = [(row, 2 * chip(d // 2) + (core + d) % 2) for d in range(1, n_col)]
 
@@ -80,7 +79,7 @@
         copy.start()
 
     barrier = pltpu.get_barrier_semaphore()
-    greeted = peers + [y_next, y_prev, z_next, z_prev]
+    greeted = peers + [y_next, y_prev, z_pair]
     for other in greeted:
         pl.semaphore_signal(barrier, inc=1, device_id=other, device_id_type=MESH)
     pl.semaphore_wait(barrier, len(greeted))
@@ -186,7 +185,7 @@
         yz_in[index, half] = [
             send(base, piece, piece, y_next),
             send(base + 1, piece, piece, y_prev),
-            send(base + 2, piece, piece, z_prev if half else z_next),
+            send(base + 2, piece, piece, z_pair),
         ]
 
     def to_partner(index, which, dx, shade):

time: 46.2 us -> 43.1 us (0.933)
  Pallas kernels: 44.4 us -> 41.3 us
    pallas_call x1, Pallas kernels: 44.4 us -> 41.3 us  [local(): pl.pallas_call(kernel, out_shape=jax.ShapeDtypeStruct((2, tile, width), B...]
where the time goes in v4:
time: 43.1 us; the launch traced here: 43 us
  Pallas kernels  41.3 us (96%)
  other arithmetic  1.63 us (4%)
    pallas_call x1, Pallas kernels, local(): pl.pallas_call(kernel, out_shape=jax.ShapeDtypeStruct((2, tile, width), B...  41.3 us
    convert_element_type x1, other arithmetic, local(): return out.reshape(user_factors.shape).astype(user_factors.dtype)  1.63 us

profile of v4, /device:TPU:1, one launch (start us, length us, event | category | flops | bytes accessed | tf_op | source)
XLA Modules:
  0.0 43.0 jit_solution(14089940363654605963)
XLA Ops:
  0.0 41.3 %shard_map.64 = bf16[2,128,256]{2,1,0:T(8,128)(2,1)} custom-call(bf16[24,128,128]{2,1,0:T(8,128)(2,1)} %conf_ref.1, s32[24]{0:T(128)} %rows_hbm.1, s32[24]{0:T(128)} %cols_hbm.1, s32[48]{0:T(128)} %owner_hbm.1, bf16[768,256]{1,0:T(8,128)(2,1)} %items_ref.1, f32[256,256]{1,0:T(8,128)} %users_ref.1), custom_call_target="tpu_custom_call" | custom-call | tf_op jit(solution)/shard_map/pallas_call | solution.py:334
  41.3 1.6 %bitcast_convert_fusion = f32[256,256]{1,0:T(8,128)} fusion(bf16[2,128,256]{2,1,0:T(8,128)(2,1)} %shard_map.64), kind=kLoop, calls=%fused_computation | loop fusion | flops 65536 | bytes 393216 | tf_op jit(solution)/shard_map/convert_element_type | solution.py:360

commit v5 on v4

--- a/solution.py
+++ b/solution.py
@@ -224,18 +224,20 @@
 
     for copy in locals_:
         copy.wait()
-    for copy in core_in + pick_in + list(conf_in.values()):
+    for copy in core_in:
+        copy.wait_recv()
+    for shard in range(n_col):
+        rows_of = slice(shard * stored, (shard + 1) * stored)
+        yt_buf[:, rows_of] = y_buf[rows_of, :].T
+
+    for copy in pick_in + list(conf_in.values()):
         copy.wait_recv()
 
     def widen(block, carry):
         wide[pl.ds(pl.multiple_of(block * part, 16), part), :] = conf_buf[block].astype(F32)
         return carry
 
-    lax.fori_loop(0, total, widen, 0, unroll=8)
-    for shard in range(n_col):
-        rows_of = slice(shard * stored, (shard + 1) * stored)
-        yt_buf[:, rows_of] = y_buf[rows_of, :].T
-
+    lax.fori_loop(0, total, widen, 0, unroll=16)
     picks = pick_buf[...].T[: 2 * all_blocks].astype(BF16)
 
     def gather(u, carry):
@@ -250,7 +252,7 @@
             p_buf[place, :] = band[:, tile:]
         return carry
 
-    lax.fori_loop(0, part, gather, 0, unroll=4)
+    lax.fori_loop(0, part, gather, 0, unroll=8)
 
     step_blocks = 2
     chunk = step_blocks * tile

time: 43.1 us -> 41.9 us (0.972)
  Pallas kernels: 41.3 us -> 40.1 us
    pallas_call x1, Pallas kernels: 41.3 us -> 40.1 us  [local(): pl.pallas_call(kernel, out_shape=jax.ShapeDtypeStruct((2, tile, width), B...]
where the time goes in v5:
time: 41.9 us; the launch traced here: 41.7 us
  Pallas kernels  40.1 us (96%)
  other arithmetic  1.63 us (4%)
    pallas_call x1, Pallas kernels, local(): pl.pallas_call(kernel, out_shape=jax.ShapeDtypeStruct((2, tile, width), B...  40.1 us
    convert_element_type x1, other arithmetic, local(): return out.reshape(user_factors.shape).astype(user_factors.dtype)  1.63 us

profile of v5, /device:TPU:1, one launch (start us, length us, event | category | flops | bytes accessed | tf_op | source)
XLA Modules:
  0.0 41.7 jit_solution(843859963645321592)
XLA Ops:
  0.0 40.1 %shard_map.64 = bf16[2,128,256]{2,1,0:T(8,128)(2,1)} custom-call(bf16[24,128,128]{2,1,0:T(8,128)(2,1)} %conf_ref.1, s32[24]{0:T(128)} %rows_hbm.1, s32[24]{0:T(128)} %cols_hbm.1, s32[48]{0:T(128)} %owner_hbm.1, bf16[768,256]{1,0:T(8,128)(2,1)} %items_ref.1, f32[256,256]{1,0:T(8,128)} %users_ref.1), custom_call_target="tpu_custom_call" | custom-call | tf_op jit(solution)/shard_map/pallas_call | solution.py:336
  40.1 1.6 %bitcast_convert_fusion = f32[256,256]{1,0:T(8,128)} fusion(bf16[2,128,256]{2,1,0:T(8,128)(2,1)} %shard_map.64), kind=kLoop, calls=%fused_computation | loop fusion | flops 65536 | bytes 393216 | tf_op jit(solution)/shard_map/convert_element_type | solution.py:362

commit v6 on v5

--- a/solution.py
+++ b/solution.py
@@ -237,7 +237,7 @@
         wide[pl.ds(pl.multiple_of(block * part, 16), part), :] = conf_buf[block].astype(F32)
         return carry
 
-    lax.fori_loop(0, total, widen, 0, unroll=16)
+    lax.fori_loop(0, total, widen, 0, unroll=32)
     picks = pick_buf[...].T[: 2 * all_blocks].astype(BF16)
 
     def gather(u, carry):
@@ -252,7 +252,7 @@
             p_buf[place, :] = band[:, tile:]
         return carry
 
-    lax.fori_loop(0, part, gather, 0, unroll=8)
+    lax.fori_loop(0, part, gather, 0, unroll=16)
 
     step_blocks = 2
     chunk = step_blocks * tile

time: 41.9 us -> 41.6 us (level)
  no operation moved by 1% of the time
where the time goes in v6:
time: 41.6 us; the launch traced here: 41.5 us
  Pallas kernels  39.9 us (96%)
  other arithmetic  1.63 us (4%)
    pallas_call x1, Pallas kernels, local(): pl.pallas_call(kernel, out_shape=jax.ShapeDtypeStruct((2, tile, width), B...  39.9 us
    convert_element_type x1, other arithmetic, local(): return out.reshape(user_factors.shape).astype(user_factors.dtype)  1.63 us

profile of v6, /device:TPU:1, one launch (start us, length us, event | category | flops | bytes accessed | tf_op | source)
XLA Modules:
  0.0 41.5 jit_solution(12225755173966368557)
XLA Ops:
  0.0 39.9 %shard_map.64 = bf16[2,128,256]{2,1,0:T(8,128)(2,1)} custom-call(bf16[24,128,128]{2,1,0:T(8,128)(2,1)} %conf_ref.1, s32[24]{0:T(128)} %rows_hbm.1, s32[24]{0:T(128)} %cols_hbm.1, s32[48]{0:T(128)} %owner_hbm.1, bf16[768,256]{1,0:T(8,128)(2,1)} %items_ref.1, f32[256,256]{1,0:T(8,128)} %users_ref.1), custom_call_target="tpu_custom_call" | custom-call | tf_op jit(solution)/shard_map/pallas_call | solution.py:336
  39.9 1.6 %bitcast_convert_fusion = f32[256,256]{1,0:T(8,128)} fusion(bf16[2,128,256]{2,1,0:T(8,128)(2,1)} %shard_map.64), kind=kLoop, calls=%fused_computation | loop fusion | flops 65536 | bytes 393216 | tf_op jit(solution)/shard_map/convert_element_type | solution.py:362
